TPU v7x, 32 devices: a whole 2x2x4 slice. The times are simulated.
32 devices in a mesh: grp: 4 (over y, core), blk: 8 (over z, x).
Axes of the slice: x: 2, y: 2, z: 4, core: 2. Of those that a mesh axis runs over, the one named last changes fastest.
Arguments:
- grads: bfloat16 [32, 256, 128], P(('grp', 'blk')), may hold values from -6 to 6
- picks: int32 [32, 256], P(('grp', 'blk')), may hold values from 0 to 511, as said below
- slot_map: int32 [32, 512], P(('grp', 'blk')), may hold values from 0 to 511, each once within a row
- momentum: float32 [16384, 128], P(('grp', 'blk')), may hold values from -6 to 6
- params: float32 [16384, 128], P(('grp', 'blk')), may hold values from -6 to 6
Outputs:
- new_momentum: float32 [16384, 128], P(('grp', 'blk'))
- new_params: float32 [16384, 128], P(('grp', 'blk'))
Inputs may be any that keep to these rules, and one draw needn't show every extreme that they name: `picks`: for each replica and owner, the 8 entries in order: the j-th lies in [j * 64, (j + 1) * 64). `slot_map`: each row is a permutation of the 512 slots.
All inputs are finite; a program needn't handle non-finite values.
Results may differ from a plain program's by a relative error of at most 0.0003.
Values may be sent and summed in bfloat16 or wider, within the bound.
A program may use at most 64 MiB of HBM per device.

v0:
```python
import jax
import jax.numpy as jnp
from jax import lax
from jax.sharding import PartitionSpec as P


def densify(values, chosen, owned):
    numbers = lax.broadcasted_iota(jnp.int32, (1, owned, 1), 1)
    onehot = (chosen[:, None, :] == numbers).astype(jnp.bfloat16)
    return jnp.einsum("nrm,nmc->nrc", onehot, values, preferred_element_type=jnp.float32)


def attach_numbers(values, chosen):
    block = values.shape[-1]
    count = chosen.shape[-1]
    upper = (chosen // 16).astype(jnp.bfloat16)
    lower = (chosen % 16).astype(jnp.bfloat16)
    filler = jnp.zeros(chosen.shape[:-1] + (block - 2 * count,), jnp.bfloat16)
    number_row = jnp.concatenate([upper, lower, filler], axis=-1)
    return jnp.concatenate([values, number_row[..., None, :]], axis=-2)


def split_numbers(packed):
    count = packed.shape[-2] - 1
    values = packed[..., :count, :]
    number_row = packed[..., count, :]
    upper = number_row[..., :count].astype(jnp.float32)
    lower = number_row[..., count : 2 * count].astype(jnp.float32)
    chosen = (upper * 16.0 + lower).astype(jnp.int32)
    return (values, chosen)


def shards(grads, picks, slot_map, momentum, params):
    groups = lax.axis_size("grp")
    columns = lax.axis_size("blk")
    block = grads.shape[-1]
    owned = slot_map.shape[1]
    values = grads.reshape(groups, columns, -1, block)
    chosen = picks.reshape(groups, columns, -1)
    packed = attach_numbers(values, chosen)
    arrived = lax.all_to_all(
        lax.all_to_all(packed, "grp", split_axis=0, concat_axis=0, tiled=True),
        "blk",
        split_axis=1,
        concat_axis=1,
        tiled=True,
    )
    arrived_values, arrived_chosen = split_numbers(arrived)
    merged = densify(arrived_values.reshape(1, -1, block), arrived_chosen.reshape(1, -1), owned)[0]
    slots = lax.broadcasted_iota(jnp.int32, (owned, owned), 0)
    placing = (slot_map[0][None, :] == slots).astype(jnp.float32)
    gradient = jnp.dot(
        placing, merged, precision=lax.Precision.HIGHEST, preferred_element_type=jnp.float32
    )
    new_momentum = 0.9 * momentum + gradient
    new_params = params - 0.05 * (gradient + 0.9 * new_momentum)
    return (new_momentum, new_params)


def solution(mesh):
    placed = (
        P(("grp", "blk"), None, None),
        P(("grp", "blk"), None),
        P(("grp", "blk"), None),
        P(("grp", "blk"), None),
        P(("grp", "blk"), None),
    )
    return jax.shard_map(
        shards,
        mesh=mesh,
        in_specs=placed,
        out_specs=(P(("grp", "blk"), None), P(("grp", "blk"), None)),
        check_vma=False,
    )
```

profile of v0, /device:TPU:0, one launch (start us, length us, event | category | flops | bytes accessed | tf_op | source)
XLA Modules:
  0.0 25.6 jit_solution(10706373403147952644)
XLA Ops:
  0.6 0.0 copy-start.4
  0.6 0.0 copy-start.2
  0.6 0.5 %broadcast.36 = s32[]{:T(128)} broadcast(s32[]{:T(128)} %constant.59), dimensions={} | broadcast | bytes 8 | tf_op args[1]
  1.2 0.1 copy-done.4
  1.3 0.7 %reduce.3 = s32[256]{0:T(256)S(1)} reduce(s32[1,256]{1,0:T(1,128)S(1)} %copy-done.4, s32[]{:T(128)} %broadcast.36), dimensions={0}, to_apply=%param.6.reduce_sub_computation.3 | reduce | bytes 2052 | tf_op args[1]
  2.0 0.1 reshape.39
  2.1 0.1 pad.4.clone
  2.2 0.1 maximum_bitcast_fusion
  2.3 0.0 copy-done.2
  2.4 8.2 %all_to_all.10 = bf16[4,8,9,128]{3,1,2,0:T(8,128)(2,1)S(1)} all-to-all(bf16[4,8,9,128]{3,1,2,0:T(8,128)(2,1)S(1)} %copy.9), channel_id=1, replica_groups=mesh['grp'=4,'blk'=8] {'grp'}, dimensions={0} | all-to-all | bytes 147456 | tf_op jit(solution)/shard_map/all_to_all | solution.py:42
  10.6 12.6 %all_to_all.11 = bf16[4,8,9,128]{3,0,2,1:T(4,128)(2,1)S(1)} all-to-all(bf16[4,8,9,128]{3,0,2,1:T(4,128)(2,1)S(1)} %copy.10), channel_id=1, replica_groups=mesh['grp'=4,'blk'=8] {'blk'}, dimensions={1} | all-to-all | bytes 147456 | tf_op jit(solution)/shard_map/all_to_all | solution.py:41
  23.2 0.0 copy-start
  23.2 0.0 copy-start.1
  23.3 0.1 add_convert_fusion
  23.3 0.1 eq.34
  23.4 0.0 copy-start.3
  23.4 0.2 fusion.2
  23.7 0.5 %copy-done = f32[512,128]{1,0:T(8,128)S(1)} copy-done((f32[512,128]{1,0:T(8,128)S(1)}, f32[512,128]{1,0:T(8,128)}, u32[]{:S(2)}) %copy-start) | copy-done | bytes 262168
  24.1 0.1 copy-done.1
  24.2 0.0 copy-done.3
  24.2 1.4 %multiply_subtract_fusion = (f32[512,128]{1,0:T(8,128)}, f32[512,128]{1,0:T(8,128)}) fusion(f32[512,128]{1,0:T(8,128)S(1)} %copy-done, f32[512,128]{1,0:T(8,128)S(1)} %copy-done.1, f32[512,128]{1,0:T(8,128)S(1)} %fusion.2, s32[512]{0:T(512)S(1)} %bitcast.13), kind=kOutput, calls=%fused_computation.5 | convolution fusion | flops 403308544 | bytes 1312768 | tf_op jit(solution)/shard_map/dot_general | solution.py:52
  (10 shorter events, 0.2 us)
Async XLA Ops:
  0.6 0.7 %copy-start.4 = (s32[1,256]{1,0:T(1,128)S(1)}, s32[1,256]{1,0:T(1,128)}, u32[]{:S(2)}) copy-start(s32[1,256]{1,0:T(1,128)} %param.6) | copy-start | bytes 3076
  0.6 1.6 %copy-start.2 = (bf16[1,256,128]{2,1,0:T(8,128)(2,1)S(1)}, bf16[1,256,128]{2,1,0:T(8,128)(2,1)}, u32[]{:S(2)}) copy-start(bf16[1,256,128]{2,1,0:T(8,128)(2,1)} %param.5) | copy-start | bytes 196612
  23.2 1.0 %copy-start = (f32[512,128]{1,0:T(8,128)S(1)}, f32[512,128]{1,0:T(8,128)}, u32[]{:S(2)}) copy-start(f32[512,128]{1,0:T(8,128)} %param.9) | copy-start | bytes 786436
  23.2 1.0 %copy-start.1 = (f32[512,128]{1,0:T(8,128)S(1)}, f32[512,128]{1,0:T(8,128)}, u32[]{:S(2)}) copy-start(f32[512,128]{1,0:T(8,128)} %param.8) | copy-start | bytes 786436
  23.4 0.8 %copy-start.3 = (s32[1,512]{1,0:T(1,128)S(1)}, s32[1,512]{1,0:T(1,128)}, u32[]{:S(2)}) copy-start(s32[1,512]{1,0:T(1,128)} %param.7) | copy-start | bytes 6148
where the time goes:
time: 25.9 us; the launch traced here: 25.6 us
  blocking collectives  20.8 us (80%)
  matrix products  1.63 us (6%)
  local copies, waits for them, and re-layouts  1.6 us (6%)
  other arithmetic  0.89 us (3%)
  between operations  0.75 us (3%)
    all_to_all x1, blocking collectives, shards(): lax.all_to_all(lax.all_to_all(packed, 'grp', split_axis=0, concat_axis=0,...  12.6 us
    all_to_all x1, blocking collectives, shards(): lax.all_to_all(packed, 'grp', split_axis=0, concat_axis=0, tiled=True)  8.2 us
    dot_general x1, matrix products, shards(): jnp.dot(placing, merged, precision=lax.Precision.HIGHEST, preferred_eleme...  1.4 us
    unnamed x13, local copies, waits for them, and re-layouts  1.25 us
    unnamed x1, other arithmetic  0.66 us

commit v1 on v0

v1 whole, which is shorter than its diff:
```python
import functools

import jax
import jax.numpy as jnp
from jax import lax
from jax.experimental import pallas as pl
from jax.experimental.pallas import tpu as pltpu
from jax.sharding import PartitionSpec as P

MESH = pl.DeviceIdType.MESH


def exchange(groups, columns, grads_hbm, picks_hbm, slots_hbm, out_ref, grads, picks, slots,
             send, recv, load_sem, send_sem, recv_sem):
    peers = groups * columns
    items, block = grads.shape
    owned = slots.shape[1]
    count = items // peers
    width = owned // count
    per_tile = block // width
    tiles = owned // block
    g = lax.axis_index("grp")
    b = lax.axis_index("blk")
    me = g * columns + b

    loads = [
        pltpu.make_async_copy(picks_hbm, picks, load_sem.at[0]),
        pltpu.make_async_copy(grads_hbm, grads, load_sem.at[1]),
        pltpu.make_async_copy(slots_hbm, slots, load_sem.at[2]),
    ]
    for load in loads:
        load.start()

    def place(k):
        other = lax.rem(me + k, peers)
        return other, (other // columns, lax.rem(other, columns))

    def each_peer(act):
        if peers <= 64:
            for k in range(1, peers):
                act(k)
        else:
            lax.fori_loop(1, peers, lambda k, c: (act(k), c)[1], 0)

    barrier = pltpu.get_barrier_semaphore()

    def greet(k):
        pl.semaphore_signal(barrier, inc=1, device_id=place(k)[1], device_id_type=MESH)

    each_peer(greet)

    loads[0].wait()
    numbers = jnp.broadcast_to(picks[...].astype(jnp.float32), (block, items)).T
    row = lax.broadcasted_iota(jnp.int32, (items, block), 0) % count
    lane = lax.broadcasted_iota(jnp.int32, (items, block), 1)
    base = (row // per_tile) * block
    hot = (numbers == (lane + base).astype(jnp.float32)).astype(jnp.float32)
    loads[1].wait()
    values = grads[...].astype(jnp.float32)
    packed = jnp.concatenate(
        [values.reshape(peers, count, block), hot.reshape(peers, count, block)], axis=1
    ).astype(jnp.bfloat16)
    send[...] = packed

    pl.semaphore_wait(barrier, peers - 1)

    def ship(k):
        other, where = place(k)
        pltpu.make_async_remote_copy(
            src_ref=send.at[other],
            dst_ref=recv.at[me],
            send_sem=send_sem,
            recv_sem=recv_sem,
            device_id=where,
            device_id_type=MESH,
        ).start()

    each_peer(ship)
    recv[me] = send[me]

    loads[2].wait()
    table = slots[...].astype(jnp.float32)
    high = jnp.floor(table * (1.0 / 256.0))
    low = table - 256.0 * high
    rows = [part[:, t * block : (t + 1) * block] for part in (low, high) for t in range(tiles)]
    rows += [jnp.zeros((1, block), jnp.float32)] * (-len(rows) % 16)
    lookup = jnp.concatenate(rows, axis=0).astype(jnp.bfloat16)

    done = pltpu.make_async_remote_copy(
        src_ref=send.at[pl.ds(0, peers - 1)],
        dst_ref=recv.at[pl.ds(0, peers - 1)],
        send_sem=send_sem,
        recv_sem=recv_sem,
        device_id=place(1)[1],
        device_id_type=MESH,
    )
    done.wait_recv()

    group = min(peers, 256 // count)
    chunk = group * count

    def part(i):
        got = recv[pl.ds(i * group, group)].astype(jnp.float32)
        vals = got[:, :count].reshape(chunk, block).astype(jnp.bfloat16)
        ones = got[:, count:].reshape(chunk, block).astype(jnp.bfloat16)
        found = lax.dot_general(
            lookup, ones, (((1,), (1,)), ((), ())), preferred_element_type=jnp.float32
        )
        where = lax.broadcasted_iota(jnp.int32, (1, chunk), 1) % count // per_tile
        slot = jnp.zeros((1, chunk), jnp.float32)
        for t in range(tiles):
            slot = jnp.where(
                where == t, found[t : t + 1] + 256.0 * found[tiles + t : tiles + t + 1], slot
            )
        number = lax.broadcasted_iota(jnp.int32, (owned, chunk), 0).astype(jnp.float32)
        put = (number == slot).astype(jnp.float32).astype(jnp.bfloat16)
        return jnp.dot(put, vals, preferred_element_type=jnp.float32)

    if peers == group:
        out_ref[...] = part(0)
    else:
        out_ref[...] = jnp.zeros_like(out_ref)

        def step(i, c):
            out_ref[...] += part(i)
            return c

        lax.fori_loop(0, peers // group, step, 0)
    done.wait_send()


def shards(grads, picks, slot_map, momentum, params):
    groups = lax.axis_size("grp")
    columns = lax.axis_size("blk")
    peers = groups * columns
    items, block = grads.shape[1:]
    owned = slot_map.shape[1]
    count = items // peers
    gradient = pl.pallas_call(
        functools.partial(exchange, groups, columns),
        out_shape=jax.ShapeDtypeStruct((owned, block), jnp.float32),
        in_specs=[pl.BlockSpec(memory_space=pl.ANY)] * 3,
        out_specs=pl.BlockSpec(memory_space=pltpu.VMEM),
        scratch_shapes=[
            pltpu.VMEM((items, block), jnp.bfloat16),
            pltpu.VMEM((1, items), jnp.int32),
            pltpu.VMEM((1, owned), jnp.int32),
            pltpu.VMEM((peers, 2 * count, block), jnp.bfloat16),
            pltpu.VMEM((peers, 2 * count, block), jnp.bfloat16),
            pltpu.SemaphoreType.DMA((3,)),
            pltpu.SemaphoreType.DMA,
            pltpu.SemaphoreType.DMA,
        ],
        compiler_params=pltpu.CompilerParams(
            collective_id=0, has_side_effects=True, vmem_limit_bytes=40 * 1024 * 1024
        ),
    )(grads[0], picks, slot_map)
    new_momentum = 0.9 * momentum + gradient
    new_params = params - 0.05 * (gradient + 0.9 * new_momentum)
    return (new_momentum, new_params)


def solution(mesh):
    placed = (
        P(("grp", "blk"), None, None),
        P(("grp", "blk"), None),
        P(("grp", "blk"), None),
        P(("grp", "blk"), None),
        P(("grp", "blk"), None),
    )
    return jax.shard_map(
        shards,
        mesh=mesh,
        in_specs=placed,
        out_specs=(P(("grp", "blk"), None), P(("grp", "blk"), None)),
        check_vma=False,
    )
```

time: 25.9 us -> 16.9 us (0.65)
  blocking collectives: 20.8 us -> 0 us
  Pallas kernels: 0 us -> 12 us
  matrix products: 1.63 us -> 0 us
  other arithmetic: 0.89 us -> 1.81 us
  local copies, waits for them, and re-layouts: 1.6 us -> 2.2 us
    all_to_all x2 -> x0, blocking collectives: 20.8 us -> none  [the longest x1 12.6 us: shards(): lax.all_to_all(lax.all_to_all(packed, 'grp', split_axis=0, concat_axis=0,...]
    pallas_call x0 -> x1, Pallas kernels: none -> 12 us  [shards(): pl.pallas_call(functools.partial(exchange, groups, columns), out_shape=ja...]
    sub x0 -> x1, other arithmetic: none -> 1.81 us  [shards(): new_params = params - 0.05 * (gradient + 0.9 * new_momentum)]
    dot_general x2 -> x0, matrix products: 1.63 us -> none  [the longest x1 1.4 us: shards(): jnp.dot(placing, merged, precision=lax.Precision.HIGHEST, preferred_eleme...]
    unnamed x13 -> x8, local copies, waits for them, and re-layouts: 1.25 us -> 2.2 us
    unnamed x1 -> x0, other arithmetic: 0.66 us -> none
where the time goes in v1:
time: 16.9 us; the launch traced here: 16.6 us
  Pallas kernels  12 us (71%)
  local copies, waits for them, and re-layouts  2.2 us (13%)
  other arithmetic  1.81 us (11%)
  between operations  0.66 us (4%)
    pallas_call x1, Pallas kernels, shards(): pl.pallas_call(functools.partial(exchange, groups, columns), out_shape=ja...  12 us
    unnamed x8, local copies, waits for them, and re-layouts  2.2 us
    sub x1, other arithmetic, shards(): new_params = params - 0.05 * (gradient + 0.9 * new_momentum)  1.81 us

profile of v1, /device:TPU:0, one launch (start us, length us, event | category | flops | bytes accessed | tf_op | source)
XLA Modules:
  0.0 16.6 jit_solution(9386935942006338735)
XLA Ops:
  0.6 0.0 copy-start.2
  0.6 0.7 %copy-done.2 = s32[1,256]{1,0:T(1,128)S(1)} copy-done((s32[1,256]{1,0:T(1,128)S(1)}, s32[1,256]{1,0:T(1,128)}, u32[]{:S(2)}) %copy-start.2) | copy-done | bytes 1048
  1.3 0.0 copy-start
  1.3 0.8 %copy-done = bf16[1,256,128]{2,1,0:T(8,128)(2,1)S(1)} copy-done((bf16[1,256,128]{2,1,0:T(8,128)(2,1)S(1)}, bf16[1,256,128]{2,1,0:T(8,128)(2,1)}, u32[]{:S(2)}) %copy-start) | copy-done | bytes 65560
  2.2 0.0 copy-start.1
  2.2 0.7 %copy-done.1 = s32[1,512]{1,0:T(1,128)S(1)} copy-done((s32[1,512]{1,0:T(1,128)S(1)}, s32[1,512]{1,0:T(1,128)}, u32[]{:S(2)}) %copy-start.1) | copy-done | bytes 2072
  2.8 0.0 copy-start.3
  2.8 12.0 %shard_map.68 = f32[512,128]{1,0:T(8,128)S(1)} custom-call(bf16[256,128]{1,0:T(8,128)(2,1)S(1)} %bitcast.1, s32[1,256]{1,0:T(1,128)S(1)} %copy-done.2, s32[1,512]{1,0:T(1,128)S(1)} %copy-done.1), custom_call_target="tpu_custom_call" | custom-call | tf_op jit(solution)/shard_map/pallas_call | solution.py:139
  14.8 0.0 copy-done.3
  14.8 1.8 %multiply_subtract_fusion = (f32[512,128]{1,0:T(8,128)}, f32[512,128]{1,0:T(8,128)}) fusion(f32[512,128]{1,0:T(8,128)S(1)} %copy-done.3, f32[512,128]{1,0:T(8,128)S(1)} %shard_map.68, f32[512,128]{1,0:T(8,128)} %param.8), kind=kLoop, calls=%fused_computation | loop fusion | flops 393216 | bytes 1310720 | tf_op jit(solution)/shard_map/sub | solution.py:159
Async XLA Ops:
  0.6 0.7 %copy-start.2 = (s32[1,256]{1,0:T(1,128)S(1)}, s32[1,256]{1,0:T(1,128)}, u32[]{:S(2)}) copy-start(s32[1,256]{1,0:T(1,128)} %picks_hbm.1) | copy-start | bytes 3076
  1.3 0.8 %copy-start = (bf16[1,256,128]{2,1,0:T(8,128)(2,1)S(1)}, bf16[1,256,128]{2,1,0:T(8,128)(2,1)}, u32[]{:S(2)}) copy-start(bf16[1,256,128]{2,1,0:T(8,128)(2,1)} %param.5) | copy-start | bytes 196612
  2.2 0.7 %copy-start.1 = (s32[1,512]{1,0:T(1,128)S(1)}, s32[1,512]{1,0:T(1,128)}, u32[]{:S(2)}) copy-start(s32[1,512]{1,0:T(1,128)} %slots_hbm.1) | copy-start | bytes 6148
  2.8 12.0 %copy-start.3 = (f32[512,128]{1,0:T(8,128)S(1)}, f32[512,128]{1,0:T(8,128)}, u32[]{:S(2)}) copy-start(f32[512,128]{1,0:T(8,128)} %param.9) | copy-start | bytes 786436

commit v2 on v1

v2 whole, which is shorter than its diff:
```python
import functools

import jax
import jax.numpy as jnp
from jax import lax
from jax.experimental import pallas as pl
from jax.experimental.pallas import tpu as pltpu
from jax.sharding import PartitionSpec as P

MESH = pl.DeviceIdType.MESH


def powers(*sizes):
    return all(size & (size - 1) == 0 for size in sizes)


def exchange(groups, columns, grads_hbm, picks_hbm, slots_hbm, momentum_hbm, params_hbm,
             recv, lookup, momentum, params, grads, picks, slots, send,
             load_sem, send_sem, recv_sem):
    peers = groups * columns
    items, block = grads.shape
    owned = slots.shape[1]
    count = items // peers
    width = owned // count
    per_tile = block // width
    tiles = owned // block
    g = lax.axis_index("grp")
    b = lax.axis_index("blk")
    me = g * columns + b

    loads = [
        pltpu.make_async_copy(source, target, load_sem.at[i])
        for i, (source, target) in enumerate(
            [
                (picks_hbm, picks),
                (grads_hbm, grads),
                (slots_hbm, slots),
                (momentum_hbm, momentum),
                (params_hbm, params),
            ]
        )
    ]
    for load in loads[:3]:
        load.start()

    def place(dg, db):
        if powers(groups, columns):
            return g ^ dg, b ^ db
        return lax.rem(g + dg, groups), lax.rem(b + db, columns)

    def each_peer(act):
        if peers <= 64:
            for db in reversed(range(columns)):
                for dg in reversed(range(groups)):
                    if dg or db:
                        act(*place(dg, db))
        else:
            def step(k, c):
                act(*place(k // columns, lax.rem(k, columns)))
                return c

            lax.fori_loop(1, peers, step, 0)

    barrier = pltpu.get_barrier_semaphore()

    def greet(og, ob):
        pl.semaphore_signal(barrier, inc=1, device_id=(og, ob), device_id_type=MESH)

    each_peer(greet)

    loads[0].wait()
    numbers = jnp.broadcast_to(picks[...].astype(jnp.float32), (block, items)).T
    row = lax.broadcasted_iota(jnp.int32, (items, block), 0) % count
    lane = lax.broadcasted_iota(jnp.int32, (items, block), 1)
    base = (row // per_tile) * block
    hot = (numbers == (lane + base).astype(jnp.float32)).astype(jnp.float32)
    loads[1].wait()
    values = grads[...].astype(jnp.float32)
    packed = jnp.concatenate(
        [values.reshape(peers, count, block), hot.reshape(peers, count, block)], axis=1
    ).astype(jnp.bfloat16)
    send[...] = packed

    pl.semaphore_wait(barrier, peers - 1)

    def ship(og, ob):
        pltpu.make_async_remote_copy(
            src_ref=send.at[og * columns + ob],
            dst_ref=recv.at[me],
            send_sem=send_sem,
            recv_sem=recv_sem,
            device_id=(og, ob),
            device_id_type=MESH,
        ).start()

    each_peer(ship)
    for load in loads[3:]:
        load.start()
    recv[me] = send[me]

    loads[2].wait()
    table = slots[...].astype(jnp.float32)
    high = jnp.floor(table * (1.0 / 256.0))
    low = table - 256.0 * high
    rows = [part[:, t * block : (t + 1) * block] for part in (low, high) for t in range(tiles)]
    rows += [jnp.zeros((1, block), jnp.float32)] * (-len(rows) % 16)
    lookup[...] = jnp.concatenate(rows, axis=0).astype(jnp.bfloat16)

    for load in loads[3:]:
        load.wait()
    done = pltpu.make_async_remote_copy(
        src_ref=send.at[pl.ds(0, peers - 1)],
        dst_ref=recv.at[pl.ds(0, peers - 1)],
        send_sem=send_sem,
        recv_sem=recv_sem,
        device_id=place(0, 1),
        device_id_type=MESH,
    )
    done.wait_recv()
    done.wait_send()


def finish(recv, lookup, momentum, params, new_momentum_hbm, new_params_hbm,
           new_momentum, new_params, total, store_sem):
    peers, twice, block = recv.shape
    count = twice // 2
    owned = momentum.shape[0]
    width = owned // count
    per_tile = block // width
    tiles = owned // block
    group = min(peers, 256 // count)
    chunk = group * count
    cut = 128

    def fetch(i):
        got = recv[pl.ds(i * group, group)].astype(jnp.float32)
        vals = got[:, :count].reshape(chunk, block).astype(jnp.bfloat16)
        ones = got[:, count:].reshape(chunk, block).astype(jnp.bfloat16)
        found = lax.dot_general(
            lookup[...], ones, (((1,), (1,)), ((), ())), preferred_element_type=jnp.float32
        )
        where = lax.broadcasted_iota(jnp.int32, (1, chunk), 1) % count // per_tile
        slot = jnp.zeros((1, chunk), jnp.float32)
        for t in range(tiles):
            slot = jnp.where(
                where == t, found[t : t + 1] + 256.0 * found[tiles + t : tiles + t + 1], slot
            )
        return vals, slot.astype(jnp.int32)

    def add_up(vals, slot, first):
        number = lax.broadcasted_iota(jnp.int32, (cut, chunk), 0) + first
        put = (number == slot).astype(jnp.float32).astype(jnp.bfloat16)
        return jnp.dot(put, vals, preferred_element_type=jnp.float32)

    single = peers == group
    if single:
        vals, slot = fetch(0)
    else:
        total[...] = jnp.zeros_like(total)

        def step(i, c):
            v, s = fetch(i)
            for first in range(0, owned, cut):
                total[pl.ds(first, cut)] += add_up(v, s, first)
            return c

        lax.fori_loop(0, peers // group, step, 0)

    stores = []
    for n, first in enumerate(range(0, owned, cut)):
        at = pl.ds(first, cut)
        gradient = add_up(vals, slot, first) if single else total[at]
        moved = 0.9 * momentum[at] + gradient
        new_momentum[at] = moved
        new_params[at] = params[at] - 0.05 * (gradient + 0.9 * moved)
        for i, (source, target) in enumerate(
            [(new_momentum, new_momentum_hbm), (new_params, new_params_hbm)]
        ):
            store = pltpu.make_async_copy(source.at[at], target.at[at], store_sem.at[2 * n + i])
            store.start()
            stores.append(store)
    for store in stores:
        store.wait()


def shards(grads, picks, slot_map, momentum, params):
    groups = lax.axis_size("grp")
    columns = lax.axis_size("blk")
    peers = groups * columns
    items, block = grads.shape[1:]
    owned = slot_map.shape[1]
    count = items // peers
    vmem = pl.BlockSpec(memory_space=pltpu.VMEM)
    hbm = pl.BlockSpec(memory_space=pltpu.HBM)
    kept = jax.ShapeDtypeStruct((owned, block), jnp.float32)
    limit = 40 * 1024 * 1024
    arrived = pl.pallas_call(
        functools.partial(exchange, groups, columns),
        out_shape=(
            jax.ShapeDtypeStruct((peers, 2 * count, block), jnp.bfloat16),
            jax.ShapeDtypeStruct((16, block), jnp.bfloat16),
            kept,
            kept,
        ),
        in_specs=[hbm] * 5,
        out_specs=(vmem,) * 4,
        scratch_shapes=[
            pltpu.VMEM((items, block), jnp.bfloat16),
            pltpu.VMEM((1, items), jnp.int32),
            pltpu.VMEM((1, owned), jnp.int32),
            pltpu.VMEM((peers, 2 * count, block), jnp.bfloat16),
            pltpu.SemaphoreType.DMA((5,)),
            pltpu.SemaphoreType.DMA,
            pltpu.SemaphoreType.DMA,
        ],
        compiler_params=pltpu.CompilerParams(
            collective_id=0, has_side_effects=True, vmem_limit_bytes=limit
        ),
    )(*[
        pltpu.with_memory_space_constraint(x, pltpu.HBM)
        for x in (grads[0], picks, slot_map, momentum, params)
    ])
    return pl.pallas_call(
        finish,
        out_shape=(kept, kept),
        in_specs=[vmem] * 4,
        out_specs=(hbm, hbm),
        scratch_shapes=[
            pltpu.VMEM((owned, block), jnp.float32),
            pltpu.VMEM((owned, block), jnp.float32),
            pltpu.VMEM((owned, block), jnp.float32),
            pltpu.SemaphoreType.DMA((2 * owned // 128,)),
        ],
        compiler_params=pltpu.CompilerParams(vmem_limit_bytes=limit),
    )(*arrived)


def solution(mesh):
    placed = (
        P(("grp", "blk"), None, None),
        P(("grp", "blk"), None),
        P(("grp", "blk"), None),
        P(("grp", "blk"), None),
        P(("grp", "blk"), None),
    )
    return jax.shard_map(
        shards,
        mesh=mesh,
        in_specs=placed,
        out_specs=(P(("grp", "blk"), None), P(("grp", "blk"), None)),
        check_vma=False,
    )
```

time: 16.9 us -> 13.5 us (0.80)
  local copies, waits for them, and re-layouts: 2.2 us -> 0 us
  other arithmetic: 1.81 us -> 0 us
  Pallas kernels: 12 us -> 12.7 us
    unnamed x8 -> x0, local copies, waits for them, and re-layouts: 2.2 us -> none
    sub x1 -> x0, other arithmetic: 1.81 us -> none  [shards(): new_params = params - 0.05 * (gradient + 0.9 * new_momentum)]
    pallas_call x1 -> x2, Pallas kernels: 12 us -> 12.7 us  [the longest x1 11.5 us: shards(): pl.pallas_call(functools.partial(exchange, groups, columns), out_shape=(j...]
where the time goes in v2:
time: 13.5 us; the launch traced here: 13.3 us
  Pallas kernels  12.7 us (94%)
  between operations  0.64 us (5%)
    pallas_call x1, Pallas kernels, shards(): pl.pallas_call(functools.partial(exchange, groups, columns), out_shape=(j...  11.5 us
    pallas_call x1, Pallas kernels, shards(): pl.pallas_call(finish, out_shape=(kept, kept), in_specs=[vmem] * 4, out_s...  1.17 us

profile of v2, /device:TPU:0, one launch (start us, length us, event | category | flops | bytes accessed | tf_op | source)
XLA Modules:
  0.0 13.3 jit_solution(11805530952088620794)
XLA Ops:
  0.6 11.5 %shard_map.68 = (bf16[32,16,128]{2,1,0:T(8,128)(2,1)S(1)}, bf16[16,128]{1,0:T(8,128)(2,1)S(1)}, f32[512,128]{1,0:T(8,128)S(1)}, f32[512,128]{1,0:T(8,128)S(1)}) custom-call(bf16[256,128]{1,0:T(8,128)(2,1)} %bitcast.1, s32[1,256]{1,0:T(1,128)} %picks_hbm.1, s32[1,512]{1,0:T(1,128)} %slots_hbm.1, f32[512,128]{1,0:T(8,128)} %momentum_hbm.1, f32[512,128]{1,0:T(8,128)} %params_hbm.1), custom_call_target="tpu_custom_call" | custom-call | tf_op jit(solution)/shard_map/pallas_call | solution.py:197
  12.1 1.2 %shard_map.69 = (f32[512,128]{1,0:T(8,128)}, f32[512,128]{1,0:T(8,128)}) custom-call(bf16[32,16,128]{2,1,0:T(8,128)(2,1)S(1)} %get-tuple-element.6.recv, bf16[16,128]{1,0:T(8,128)(2,1)S(1)} %get-tuple-element.7.lookup, f32[512,128]{1,0:T(8,128)S(1)} %get-tuple-element.8.momentum, f32[512,128]{1,0:T(8,128)S(1)} %get-tuple-element.9.params), custom_call_target="tpu_custom_call" | custom-call | tf_op jit(solution)/shard_map/pallas_call | solution.py:223

commit v3 on v2

--- a/solution.py
+++ b/solution.py
@@ -22,8 +22,6 @@
     owned = slots.shape[1]
     count = items // peers
     width = owned // count
-    per_tile = block // width
-    tiles = owned // block
     g = lax.axis_index("grp")
     b = lax.axis_index("blk")
     me = g * columns + b
@@ -69,17 +67,21 @@
     each_peer(greet)
 
     loads[0].wait()
+    halves = block // width
+    rows = count // halves
     numbers = jnp.broadcast_to(picks[...].astype(jnp.float32), (block, items)).T
-    row = lax.broadcasted_iota(jnp.int32, (items, block), 0) % count
-    lane = lax.broadcasted_iota(jnp.int32, (items, block), 1)
-    base = (row // per_tile) * block
-    hot = (numbers == (lane + base).astype(jnp.float32)).astype(jnp.float32)
+    numbers = numbers.reshape(peers, halves, rows, block)
+    lane = lax.broadcasted_iota(jnp.int32, (peers, rows, block), 2)
+    row = lax.broadcasted_iota(jnp.int32, (peers, rows, block), 1)
+    half = lane // width
+    target = (lane % width + (row + rows * half) * width).astype(jnp.float32)
+    number = numbers[:, 0]
+    for h in range(1, halves):
+        number = jnp.where(half == h, numbers[:, h], number)
+    send[:, halves] = (number == target).astype(jnp.float32).astype(jnp.bfloat16)
     loads[1].wait()
-    values = grads[...].astype(jnp.float32)
-    packed = jnp.concatenate(
-        [values.reshape(peers, count, block), hot.reshape(peers, count, block)], axis=1
-    ).astype(jnp.bfloat16)
-    send[...] = packed
+    values = grads[...].astype(jnp.float32).reshape(peers, halves, rows, block)
+    send[:, :halves] = values.astype(jnp.bfloat16)
 
     pl.semaphore_wait(barrier, peers - 1)
 
@@ -102,9 +104,15 @@
     table = slots[...].astype(jnp.float32)
     high = jnp.floor(table * (1.0 / 256.0))
     low = table - 256.0 * high
-    rows = [part[:, t * block : (t + 1) * block] for part in (low, high) for t in range(tiles)]
-    rows += [jnp.zeros((1, block), jnp.float32)] * (-len(rows) % 16)
-    lookup[...] = jnp.concatenate(rows, axis=0).astype(jnp.bfloat16)
+    blank = jnp.zeros((1, width), jnp.float32)
+    entries = []
+    for part in (low, high):
+        for j in range(count):
+            mine = part[:, j * width : (j + 1) * width]
+            entries.append(
+                jnp.concatenate([mine if h == j // rows else blank for h in range(halves)], axis=1)
+            )
+    lookup[...] = jnp.concatenate(entries, axis=0).astype(jnp.bfloat16)
 
     for load in loads[3:]:
         load.wait()
@@ -122,30 +130,31 @@
 
 def finish(recv, lookup, momentum, params, new_momentum_hbm, new_params_hbm,
            new_momentum, new_params, total, store_sem):
-    peers, twice, block = recv.shape
-    count = twice // 2
+    peers, parts, rows, block = recv.shape
+    halves = parts - 1
+    count = halves * rows
     owned = momentum.shape[0]
-    width = owned // count
-    per_tile = block // width
-    tiles = owned // block
     group = min(peers, 256 // count)
     chunk = group * count
     cut = 128
 
     def fetch(i):
         got = recv[pl.ds(i * group, group)].astype(jnp.float32)
-        vals = got[:, :count].reshape(chunk, block).astype(jnp.bfloat16)
-        ones = got[:, count:].reshape(chunk, block).astype(jnp.bfloat16)
+        flat = [got[:, h].reshape(group * rows, block) for h in range(parts)]
+        vals = jnp.concatenate(flat[:halves], axis=0).astype(jnp.bfloat16)
         found = lax.dot_general(
-            lookup[...], ones, (((1,), (1,)), ((), ())), preferred_element_type=jnp.float32
+            lookup[...], flat[halves].astype(jnp.bfloat16), (((1,), (1,)), ((), ())),
+            preferred_element_type=jnp.float32,
         )
-        where = lax.broadcasted_iota(jnp.int32, (1, chunk), 1) % count // per_tile
-        slot = jnp.zeros((1, chunk), jnp.float32)
-        for t in range(tiles):
-            slot = jnp.where(
-                where == t, found[t : t + 1] + 256.0 * found[tiles + t : tiles + t + 1], slot
-            )
-        return vals, slot.astype(jnp.int32)
+        found = found[:count] + 256.0 * found[count:]
+        where = lax.broadcasted_iota(jnp.int32, (1, group * rows), 1) % rows
+        slots = []
+        for h in range(halves):
+            slot = found[h * rows : h * rows + 1]
+            for r in range(1, rows):
+                slot = jnp.where(where == r, found[h * rows + r : h * rows + r + 1], slot)
+            slots.append(slot)
+        return vals, jnp.concatenate(slots, axis=1).astype(jnp.int32)
 
     def add_up(vals, slot, first):
         number = lax.broadcasted_iota(jnp.int32, (cut, chunk), 0) + first
@@ -190,6 +199,8 @@
     items, block = grads.shape[1:]
     owned = slot_map.shape[1]
     count = items // peers
+    halves = block * count // owned
+    shape = (peers, halves + 1, count // halves, block)
     vmem = pl.BlockSpec(memory_space=pltpu.VMEM)
     hbm = pl.BlockSpec(memory_space=pltpu.HBM)
     kept = jax.ShapeDtypeStruct((owned, block), jnp.float32)
@@ -197,8 +208,8 @@
     arrived = pl.pallas_call(
         functools.partial(exchange, groups, columns),
         out_shape=(
-            jax.ShapeDtypeStruct((peers, 2 * count, block), jnp.bfloat16),
-            jax.ShapeDtypeStruct((16, block), jnp.bfloat16),
+            jax.ShapeDtypeStruct(shape, jnp.bfloat16),
+            jax.ShapeDtypeStruct((2 * count, block), jnp.bfloat16),
             kept,
             kept,
         ),
@@ -208,7 +219,7 @@
             pltpu.VMEM((items, block), jnp.bfloat16),
             pltpu.VMEM((1, items), jnp.int32),
             pltpu.VMEM((1, owned), jnp.int32),
-            pltpu.VMEM((peers, 2 * count, block), jnp.bfloat16),
+            pltpu.VMEM(shape, jnp.bfloat16),
             pltpu.SemaphoreType.DMA((5,)),
             pltpu.SemaphoreType.DMA,
             pltpu.SemaphoreType.DMA,

time: 13.5 us -> 12.8 us (0.948)
  Pallas kernels: 12.7 us -> 12 us
    pallas_call x1, Pallas kernels: 11.5 us -> 10.8 us  [shards(): pl.pallas_call(functools.partial(exchange, groups, columns), out_shape=(j...]
where the time goes in v3:
time: 12.8 us; the launch traced here: 12.6 us
  Pallas kernels  12 us (94%)
  between operations  0.64 us (5%)
    pallas_call x1, Pallas kernels, shards(): pl.pallas_call(functools.partial(exchange, groups, columns), out_shape=(j...  10.8 us
    pallas_call x1, Pallas kernels, shards(): pl.pallas_call(finish, out_shape=(kept, kept), in_specs=[vmem] * 4, out_s...  1.18 us

profile of v3, /device:TPU:0, one launch (start us, length us, event | category | flops | bytes accessed | tf_op | source)
XLA Modules:
  0.0 12.6 jit_solution(13809269031427522772)
XLA Ops:
  0.6 10.8 %shard_map.68 = (bf16[32,3,4,128]{3,2,1,0:T(4,128)(2,1)S(1)}, bf16[16,128]{1,0:T(8,128)(2,1)S(1)}, f32[512,128]{1,0:T(8,128)S(1)}, f32[512,128]{1,0:T(8,128)S(1)}) custom-call(bf16[256,128]{1,0:T(8,128)(2,1)} %bitcast.1, s32[1,256]{1,0:T(1,128)} %picks_hbm.1, s32[1,512]{1,0:T(1,128)} %slots_hbm.1, f32[512,128]{1,0:T(8,128)} %momentum_hbm.1, ...), custom_call_target="tpu_custom_call" | custom-call | tf_op jit(solution)/shard_map/pallas_call | solution.py:208
  11.4 1.2 %shard_map.69 = (f32[512,128]{1,0:T(8,128)}, f32[512,128]{1,0:T(8,128)}) custom-call(bf16[32,3,4,128]{3,2,1,0:T(4,128)(2,1)S(1)} %get-tuple-element.6.recv, bf16[16,128]{1,0:T(8,128)(2,1)S(1)} %get-tuple-element.7.lookup, f32[512,128]{1,0:T(8,128)S(1)} %get-tuple-element.8.momentum, f32[512,128]{1,0:T(8,128)S(1)} %get-tuple-element.9.params), custom_call_target="tpu_custom_call" | custom-call | tf_op jit(solution)/shard_map/pallas_call | solution.py:234

commit v4 on v3

--- a/solution.py
+++ b/solution.py
@@ -7,7 +7,7 @@
 from jax.experimental.pallas import tpu as pltpu
 from jax.sharding import PartitionSpec as P
 
-MESH = pl.DeviceIdType.MESH
+LOGICAL = pl.DeviceIdType.LOGICAL
 
 
 def powers(*sizes):
@@ -41,28 +41,26 @@
     for load in loads[:3]:
         load.start()
 
-    def place(dg, db):
-        if powers(groups, columns):
-            return g ^ dg, b ^ db
-        return lax.rem(g + dg, groups), lax.rem(b + db, columns)
+    def place(k):
+        return me ^ k if powers(peers) else lax.rem(me + k, peers)
 
     def each_peer(act):
         if peers <= 64:
             for db in reversed(range(columns)):
                 for dg in reversed(range(groups)):
                     if dg or db:
-                        act(*place(dg, db))
+                        act(place(dg * columns + db))
         else:
             def step(k, c):
-                act(*place(k // columns, lax.rem(k, columns)))
+                act(place(k))
                 return c
 
             lax.fori_loop(1, peers, step, 0)
 
     barrier = pltpu.get_barrier_semaphore()
 
-    def greet(og, ob):
-        pl.semaphore_signal(barrier, inc=1, device_id=(og, ob), device_id_type=MESH)
+    def greet(other):
+        pl.semaphore_signal(barrier, inc=1, device_id=other, device_id_type=LOGICAL)
 
     each_peer(greet)
 
@@ -85,14 +83,14 @@
 
     pl.semaphore_wait(barrier, peers - 1)
 
-    def ship(og, ob):
+    def ship(other):
         pltpu.make_async_remote_copy(
-            src_ref=send.at[og * columns + ob],
+            src_ref=send.at[other],
             dst_ref=recv.at[me],
             send_sem=send_sem,
             recv_sem=recv_sem,
-            device_id=(og, ob),
-            device_id_type=MESH,
+            device_id=other,
+            device_id_type=LOGICAL,
         ).start()
 
     each_peer(ship)
@@ -121,8 +119,8 @@
         dst_ref=recv.at[pl.ds(0, peers - 1)],
         send_sem=send_sem,
         recv_sem=recv_sem,
-        device_id=place(0, 1),
-        device_id_type=MESH,
+        device_id=place(1),
+        device_id_type=LOGICAL,
     )
     done.wait_recv()
     done.wait_send()

time: 12.8 us -> 12.8 us (level)
  no operation moved by 1% of the time
where the time goes in v4:
time: 12.8 us; the launch traced here: 12.6 us
  Pallas kernels  12 us (94%)
  between operations  0.64 us (5%)
    pallas_call x1, Pallas kernels, shards(): pl.pallas_call(functools.partial(exchange, groups, columns), out_shape=(j...  10.8 us
    pallas_call x1, Pallas kernels, shards(): pl.pallas_call(finish, out_shape=(kept, kept), in_specs=[vmem] * 4, out_s...  1.17 us

profile of v4, /device:TPU:0, one launch (start us, length us, event | category | flops | bytes accessed | tf_op | source)
XLA Modules:
  0.0 12.6 jit_solution(13283651197587807023)
XLA Ops:
  0.6 10.8 %shard_map.68 = (bf16[32,3,4,128]{3,2,1,0:T(4,128)(2,1)S(1)}, bf16[16,128]{1,0:T(8,128)(2,1)S(1)}, f32[512,128]{1,0:T(8,128)S(1)}, f32[512,128]{1,0:T(8,128)S(1)}) custom-call(bf16[256,128]{1,0:T(8,128)(2,1)} %bitcast.1, s32[1,256]{1,0:T(1,128)} %picks_hbm.1, s32[1,512]{1,0:T(1,128)} %slots_hbm.1, f32[512,128]{1,0:T(8,128)} %momentum_hbm.1, ...), custom_call_target="tpu_custom_call" | custom-call | tf_op jit(solution)/shard_map/pallas_call | solution.py:206
  11.4 1.2 %shard_map.69 = (f32[512,128]{1,0:T(8,128)}, f32[512,128]{1,0:T(8,128)}) custom-call(bf16[32,3,4,128]{3,2,1,0:T(4,128)(2,1)S(1)} %get-tuple-element.6.recv, bf16[16,128]{1,0:T(8,128)(2,1)S(1)} %get-tuple-element.7.lookup, f32[512,128]{1,0:T(8,128)S(1)} %get-tuple-element.8.momentum, f32[512,128]{1,0:T(8,128)S(1)} %get-tuple-element.9.params), custom_call_target="tpu_custom_call" | custom-call | tf_op jit(solution)/shard_map/pallas_call | solution.py:232

commit v5 on v4

--- a/solution.py
+++ b/solution.py
@@ -63,6 +63,8 @@
         pl.semaphore_signal(barrier, inc=1, device_id=other, device_id_type=LOGICAL)
 
     each_peer(greet)
+    for load in loads[3:]:
+        load.start()
 
     loads[0].wait()
     halves = block // width
@@ -94,8 +96,6 @@
         ).start()
 
     each_peer(ship)
-    for load in loads[3:]:
-        load.start()
     recv[me] = send[me]
 
     loads[2].wait()

time: 12.8 us -> 12.7 us (level)
  no operation moved by 1% of the time
where the time goes in v5:
time: 12.7 us; the launch traced here: 12.6 us
  Pallas kernels  12 us (94%)
  between operations  0.64 us (5%)
    pallas_call x1, Pallas kernels, shards(): pl.pallas_call(functools.partial(exchange, groups, columns), out_shape=(j...  10.8 us
    pallas_call x1, Pallas kernels, shards(): pl.pallas_call(finish, out_shape=(kept, kept), in_specs=[vmem] * 4, out_s...  1.17 us

profile of v5, /device:TPU:0, one launch (start us, length us, event | category | flops | bytes accessed | tf_op | source)
XLA Modules:
  0.0 12.6 jit_solution(11276788864301202277)
XLA Ops:
  0.6 10.8 %shard_map.68 = (bf16[32,3,4,128]{3,2,1,0:T(4,128)(2,1)S(1)}, bf16[16,128]{1,0:T(8,128)(2,1)S(1)}, f32[512,128]{1,0:T(8,128)S(1)}, f32[512,128]{1,0:T(8,128)S(1)}) custom-call(bf16[256,128]{1,0:T(8,128)(2,1)} %bitcast.1, s32[1,256]{1,0:T(1,128)} %picks_hbm.1, s32[1,512]{1,0:T(1,128)} %slots_hbm.1, f32[512,128]{1,0:T(8,128)} %momentum_hbm.1, ...), custom_call_target="tpu_custom_call" | custom-call | tf_op jit(solution)/shard_map/pallas_call | solution.py:206
  11.4 1.2 %shard_map.69 = (f32[512,128]{1,0:T(8,128)}, f32[512,128]{1,0:T(8,128)}) custom-call(bf16[32,3,4,128]{3,2,1,0:T(4,128)(2,1)S(1)} %get-tuple-element.6.recv, bf16[16,128]{1,0:T(8,128)(2,1)S(1)} %get-tuple-element.7.lookup, f32[512,128]{1,0:T(8,128)S(1)} %get-tuple-element.8.momentum, f32[512,128]{1,0:T(8,128)S(1)} %get-tuple-element.9.params), custom_call_target="tpu_custom_call" | custom-call | tf_op jit(solution)/shard_map/pallas_call | solution.py:232

commit v6 on v4

--- a/solution.py
+++ b/solution.py
@@ -134,7 +134,7 @@
     owned = momentum.shape[0]
     group = min(peers, 256 // count)
     chunk = group * count
-    cut = 128
+    cut = 256
 
     def fetch(i):
         got = recv[pl.ds(i * group, group)].astype(jnp.float32)
@@ -238,7 +238,7 @@
             pltpu.VMEM((owned, block), jnp.float32),
             pltpu.VMEM((owned, block), jnp.float32),
             pltpu.VMEM((owned, block), jnp.float32),
-            pltpu.SemaphoreType.DMA((2 * owned // 128,)),
+            pltpu.SemaphoreType.DMA((2 * owned // 256,)),
         ],
         compiler_params=pltpu.CompilerParams(vmem_limit_bytes=limit),
     )(*arrived)

time: 12.8 us -> 12.8 us (level)
  no operation moved by 1% of the time
where the time goes in v6:
time: 12.8 us; the launch traced here: 12.6 us
  Pallas kernels  12 us (94%)
  between operations  0.64 us (5%)
    pallas_call x1, Pallas kernels, shards(): pl.pallas_call(functools.partial(exchange, groups, columns), out_shape=(j...  10.8 us
    pallas_call x1, Pallas kernels, shards(): pl.pallas_call(finish, out_shape=(kept, kept), in_specs=[vmem] * 4, out_s...  1.19 us

profile of v6, /device:TPU:0, one launch (start us, length us, event | category | flops | bytes accessed | tf_op | source)
XLA Modules:
  0.0 12.6 jit_solution(1801392782966541839)
XLA Ops:
  0.6 10.8 %shard_map.68 = (bf16[32,3,4,128]{3,2,1,0:T(4,128)(2,1)S(1)}, bf16[16,128]{1,0:T(8,128)(2,1)S(1)}, f32[512,128]{1,0:T(8,128)S(1)}, f32[512,128]{1,0:T(8,128)S(1)}) custom-call(bf16[256,128]{1,0:T(8,128)(2,1)} %bitcast.1, s32[1,256]{1,0:T(1,128)} %picks_hbm.1, s32[1,512]{1,0:T(1,128)} %slots_hbm.1, f32[512,128]{1,0:T(8,128)} %momentum_hbm.1, ...), custom_call_target="tpu_custom_call" | custom-call | tf_op jit(solution)/shard_map/pallas_call | solution.py:206
  11.4 1.2 %shard_map.69 = (f32[512,128]{1,0:T(8,128)}, f32[512,128]{1,0:T(8,128)}) custom-call(bf16[32,3,4,128]{3,2,1,0:T(4,128)(2,1)S(1)} %get-tuple-element.6.recv, bf16[16,128]{1,0:T(8,128)(2,1)S(1)} %get-tuple-element.7.lookup, f32[512,128]{1,0:T(8,128)S(1)} %get-tuple-element.8.momentum, f32[512,128]{1,0:T(8,128)S(1)} %get-tuple-element.9.params), custom_call_target="tpu_custom_call" | custom-call | tf_op jit(solution)/shard_map/pallas_call | solution.py:232

commit v7 on v6

--- a/solution.py
+++ b/solution.py
@@ -46,8 +46,8 @@
 
     def each_peer(act):
         if peers <= 64:
-            for db in reversed(range(columns)):
-                for dg in reversed(range(groups)):
+            for dg in reversed(range(groups)):
+                for db in reversed(range(columns)):
                     if dg or db:
                         act(place(dg * columns + db))
         else:

time: 12.8 us -> 12.7 us (level)
  no operation moved by 1% of the time
where the time goes in v7:
time: 12.7 us; the launch traced here: 12.5 us
  Pallas kernels  11.9 us (94%)
  between operations  0.64 us (5%)
    pallas_call x1, Pallas kernels, shards(): pl.pallas_call(functools.partial(exchange, groups, columns), out_shape=(j...  10.7 us
    pallas_call x1, Pallas kernels, shards(): pl.pallas_call(finish, out_shape=(kept, kept), in_specs=[vmem] * 4, out_s...  1.19 us

profile of v7, /device:TPU:0, one launch (start us, length us, event | category | flops | bytes accessed | tf_op | source)
XLA Modules:
  0.0 12.5 jit_solution(13185362121429029923)
XLA Ops:
  0.6 10.7 %shard_map.68 = (bf16[32,3,4,128]{3,2,1,0:T(4,128)(2,1)S(1)}, bf16[16,128]{1,0:T(8,128)(2,1)S(1)}, f32[512,128]{1,0:T(8,128)S(1)}, f32[512,128]{1,0:T(8,128)S(1)}) custom-call(bf16[256,128]{1,0:T(8,128)(2,1)} %bitcast.1, s32[1,256]{1,0:T(1,128)} %picks_hbm.1, s32[1,512]{1,0:T(1,128)} %slots_hbm.1, f32[512,128]{1,0:T(8,128)} %momentum_hbm.1, ...), custom_call_target="tpu_custom_call" | custom-call | tf_op jit(solution)/shard_map/pallas_call | solution.py:206
  11.3 1.2 %shard_map.69 = (f32[512,128]{1,0:T(8,128)}, f32[512,128]{1,0:T(8,128)}) custom-call(bf16[32,3,4,128]{3,2,1,0:T(4,128)(2,1)S(1)} %get-tuple-element.6.recv, bf16[16,128]{1,0:T(8,128)(2,1)S(1)} %get-tuple-element.7.lookup, f32[512,128]{1,0:T(8,128)S(1)} %get-tuple-element.8.momentum, f32[512,128]{1,0:T(8,128)S(1)} %get-tuple-element.9.params), custom_call_target="tpu_custom_call" | custom-call | tf_op jit(solution)/shard_map/pallas_call | solution.py:232
